TPU v7x, 128 devices: a whole 4x4x4 slice. The times are simulated.
128 devices in a mesh: dp: 16 (over x, z_lo, core), owner: 8 (over y, z_hi).
Axes of the slice: x: 4, y: 4, z: 4 (z_hi: 2, z_lo: 2; z = z_hi * 2 + z_lo), core: 2. Of those that a mesh axis runs over, the one named last changes fastest.
Arguments:
- layer_inputs: bfloat16 [16384, 5120], P(('dp', 'owner')), may hold values from -200 to 200
- output_grads: bfloat16 [16384, 13824], P(('dp', 'owner')), may hold values from -200 to 200
- weight_grad: bfloat16 [5120, 13824], P('dp', 'owner'), may hold values from -0.15625 to 0.15625
Outputs:
- preconditioned: bfloat16 [5120, 13824], P('dp')
All inputs are finite; a program needn't handle non-finite values.
Results may differ from a plain program's by a relative error of at most 0.017.
Values may be sent and summed in bfloat16 or wider, within the bound.
No kernel may reach another device: no remote copies, remote signals or barrier semaphores. Data moves between devices by JAX's collectives and lax.ppermute only.
A program may use at most 128 MiB of HBM per device.

v0:
```python
import jax
import jax.numpy as jnp
from jax import lax
from jax.sharding import PartitionSpec as P

BA = 320
BG = 864


damping = 0.1


def factor_blocks(rows, size):
    count = rows.shape[1] // size
    pieces = rows.reshape(rows.shape[0], count, size)
    return lax.dot_general(
        pieces, pieces, (((0,), (0,)), ((1,), (1,))), preferred_element_type=jnp.float32
    )


def damped_inverse(factor):
    size = factor.shape[-1]
    identity = jnp.eye(size, dtype=jnp.float32)
    lower = jnp.linalg.cholesky(factor + damping * identity)
    target = jnp.broadcast_to(identity, factor.shape)
    return jax.scipy.linalg.cho_solve((lower, True), target).astype(jnp.bfloat16)


def shards(layer_inputs, output_grads, weight_grad):
    total_tokens = layer_inputs.shape[0] * lax.axis_size("dp") * lax.axis_size("owner")
    local_sums = factor_blocks(layer_inputs, BA)
    partial_value = lax.psum_scatter(local_sums, "dp", scatter_dimension=0, tiled=True)
    act_factor = lax.psum(partial_value, "owner") / total_tokens
    unit_rows = lax.all_to_all(output_grads, "owner", split_axis=1, concat_axis=0, tiled=True)
    grad_factor = lax.psum(factor_blocks(unit_rows, BG), "dp") / total_tokens
    act_inverse = damped_inverse(act_factor)
    grad_inverse = damped_inverse(grad_factor)
    height, width = weight_grad.shape
    stacked = weight_grad.reshape(act_inverse.shape[0], BA, width)
    left = lax.dot_general(
        act_inverse, stacked, (((2,), (1,)), ((0,), (0,))), preferred_element_type=jnp.float32
    )
    left = left.astype(jnp.bfloat16).reshape(height, width)
    right = jnp.einsum(
        "rkb,kbc->rkc",
        left.reshape(height, grad_inverse.shape[0], BG),
        grad_inverse,
        preferred_element_type=jnp.float32,
    )
    result = right.astype(jnp.bfloat16).reshape(height, width)
    return lax.all_gather(result, "owner", axis=1, tiled=True)


def solution(mesh):
    in_specs = (P(("dp", "owner"), None), P(("dp", "owner"), None), P("dp", "owner"))
    out_specs = P("dp", None)
    return jax.shard_map(shards, mesh=mesh, in_specs=in_specs, out_specs=out_specs, check_vma=False)
```

profile of v0, /device:TPU:33, one launch (start us, length us, event | category | flops | bytes accessed | tf_op | source)
XLA Modules:
  0.0 1179.4 jit_solution(6196435849423772369)
XLA Ops:
  6.5 6.0 copy.185
  12.6 49.3 %all_to_all.16 = bf16[128,8,1728]{0,2,1:T(8,128)(2,1)S(1)} all-to-all(bf16[128,8,1728]{0,2,1:T(8,128)(2,1)} %bitcast.235), channel_id=1, replica_groups=mesh['dp'=16,'owner'=8] {'owner'}, dimensions={1} | all-to-all | bytes 7077888 | tf_op jit(solution)/shard_map/all_to_all | solution.py:34
  61.9 11.2 copy.186
  73.1 6.6 reshape.321
  79.7 9.6 fusion.163
  91.1 4.4 fusion.164
  102.9 137.0 %all-reduce.9.cloned.1.call-done = f32[2,864,864]{1,2,0:T(8,128)} async-done(((f32[2,864,864]{1,2,0:T(8,128)}), f32[2,864,864]{1,2,0:T(8,128)}) %all-reduce.9.cloned.1.call-update) | async-done | bytes 5971984 | tf_op jit(solution)/shard_map/psum | solution.py:35
  239.9 6.8 multiply_add_fusion
  246.6 7.3 copy.188
  253.9 6.7 fusion
  263.2 23.5 %custom-call.94 = f32[2,128,128]{2,1,0:T(8,128)S(1)} custom-call(f32[2,128,128]{2,1,0:T(8,128)S(1)} %cholesky.704), custom_call_target="Cholesky" | custom-call | tf_op jit(solution)/shard_map/jit(cholesky)/cholesky | solution.py:24
  286.7 19.7 %custom-call.95 = f32[2,1,128,128]{2,3,1,0:T(8,128)S(1)} custom-call(f32[2,1,128,128]{3,2,1,0:T(8,128)S(1)} %select_bitcast_fusion.5), custom_call_target="InvertDiagBlocksLowerTriangular" | custom-call | tf_op jit(solution)/shard_map/jit(cholesky)/cholesky | solution.py:24
  314.8 25.1 %custom-call.96 = f32[2,128,128]{2,1,0:T(8,128)} custom-call(f32[2,128,128]{2,1,0:T(8,128)} %cholesky.708), custom_call_target="Cholesky" | custom-call | tf_op jit(solution)/shard_map/jit(cholesky)/cholesky | solution.py:24
  341.6 21.1 %custom-call.97 = f32[2,1,128,128]{2,3,1,0:T(8,128)} custom-call(f32[2,1,128,128]{3,2,1,0:T(8,128)} %get-tuple-element.71), custom_call_target="InvertDiagBlocksLowerTriangular" | custom-call | tf_op jit(solution)/shard_map/jit(cholesky)/cholesky | solution.py:24
  368.6 24.3 %custom-call.98 = f32[2,128,128]{2,1,0:T(8,128)S(1)} custom-call(f32[2,128,128]{2,1,0:T(8,128)} %cholesky.713), custom_call_target="Cholesky" | custom-call | tf_op jit(solution)/shard_map/jit(cholesky)/cholesky | solution.py:24
  393.6 21.3 %custom-call.99 = f32[2,1,128,128]{2,3,1,0:T(8,128)} custom-call(f32[2,1,128,128]{3,2,1,0:T(8,128)} %get-tuple-element.69), custom_call_target="InvertDiagBlocksLowerTriangular" | custom-call | tf_op jit(solution)/shard_map/jit(cholesky)/cholesky | solution.py:24
  417.2 3.1 fusion.64
  421.0 24.9 %custom-call.100 = f32[2,128,128]{2,1,0:T(8,128)} custom-call(f32[2,128,128]{2,1,0:T(8,128)} %cholesky.718), custom_call_target="Cholesky" | custom-call | tf_op jit(solution)/shard_map/jit(cholesky)/cholesky | solution.py:24
  447.6 21.5 %custom-call.101 = f32[2,1,128,128]{2,3,1,0:T(8,128)} custom-call(f32[2,1,128,128]{3,2,1,0:T(8,128)} %get-tuple-element.67), custom_call_target="InvertDiagBlocksLowerTriangular" | custom-call | tf_op jit(solution)/shard_map/jit(cholesky)/cholesky | solution.py:24
  474.9 24.9 %custom-call.102 = f32[2,128,128]{2,1,0:T(8,128)} custom-call(f32[2,128,128]{2,1,0:T(8,128)} %cholesky.723), custom_call_target="Cholesky" | custom-call | tf_op jit(solution)/shard_map/jit(cholesky)/cholesky | solution.py:24
  501.4 21.1 %custom-call.103 = f32[2,1,128,128]{2,3,1,0:T(8,128)} custom-call(f32[2,1,128,128]{3,2,1,0:T(8,128)} %get-tuple-element.65), custom_call_target="InvertDiagBlocksLowerTriangular" | custom-call | tf_op jit(solution)/shard_map/jit(cholesky)/cholesky | solution.py:24
  527.9 24.4 %custom-call.104 = f32[2,128,128]{2,1,0:T(8,128)S(1)} custom-call(f32[2,128,128]{2,1,0:T(8,128)} %cholesky.728), custom_call_target="Cholesky" | custom-call | tf_op jit(solution)/shard_map/jit(cholesky)/cholesky | solution.py:24
  554.1 20.5 %custom-call.105 = f32[2,1,128,128]{2,3,1,0:T(8,128)S(1)} custom-call(f32[2,1,128,128]{3,2,1,0:T(8,128)} %get-tuple-element.63), custom_call_target="InvertDiagBlocksLowerTriangular" | custom-call | tf_op jit(solution)/shard_map/jit(cholesky)/cholesky | solution.py:24
  577.5 17.6 %custom-call.106 = f32[2,96,96]{2,1,0:T(8,128)S(1)} custom-call(f32[2,96,96]{2,1,0:T(8,128)S(1)} %convolution_subtract_fusion.13), custom_call_target="Cholesky" | custom-call | tf_op jit(solution)/shard_map/jit(cholesky)/cholesky | solution.py:24
  596.4 3.7 select_select_fusion
  602.7 22.3 %while.4 = (s32[]{:T(128)}, f32[2,864,864]{2,1,0:T(8,128)}, s32[6,2]{0,1:T(2,128)S(1)}, f32[6,2,128,128]{3,2,0,1:T(8,128)}) while((s32[]{:T(128)}, f32[2,864,864]{2,1,0:T(8,128)}, s32[6,2]{0,1:T(2,128)S(1)}, f32[6,2,128,128]{3,2,0,1:T(8,128)}) %tuple.99), condition=%wide.while_cond.clone, body=%wide.while_body.sunk.clone | while | flops 2 | bytes 263269 | solution.py:26
  627.1 138.8 %custom-call.107 = f32[2,7,128,128]{2,3,1,0:T(8,128)S(1)} custom-call(f32[2,7,128,128]{3,2,1,0:T(8,128)} %pad_maximum_fusion), custom_call_target="InvertDiagBlocksLowerTriangular" | custom-call | tf_op jit(solution)/shard_map/jit(_cho_solve)/vmap()/triangular_solve | solution.py:26
  775.3 4.0 fusion.53
  780.3 4.5 fusion.59
  786.9 5.4 convolution_subtract_fusion.3
  794.1 6.2 convolution_subtract_fusion.6
  802.2 3.1 convolution_subtract_fusion.2
  811.0 3.9 fusion.50
  815.7 4.1 fusion.56
  821.1 5.8 convolution_subtract_fusion.1
  828.1 5.8 convolution_subtract_fusion
  841.4 79.8 %all-reduce.11.cloned.1.call-done = f32[1,320,320]{2,1,0:T(8,128)} async-done(((f32[1,320,320]{2,1,0:T(8,128)}), f32[1,320,320]{2,1,0:T(8,128)}) %all-reduce.11.cloned.1.call-update) | async-done | bytes 409616 | tf_op jit(solution)/shard_map/psum | solution.py:33
  923.7 11.7 custom-call.108
  935.5 9.8 custom-call.109
  945.8 11.7 custom-call.110
  957.6 10.0 custom-call.111
  968.0 5.8 custom-call.112
  977.3 5.3 while.5
  983.7 29.5 %custom-call.113 = f32[3,128,128]{1,2,0:T(8,128)S(1)} custom-call(f32[3,128,128]{2,1,0:T(8,128)S(1)} %pad_maximum_fusion.1), custom_call_target="InvertDiagBlocksLowerTriangular" | custom-call | tf_op jit(solution)/shard_map/jit(_cho_solve)/triangular_solve | solution.py:26
  1019.5 3.4 fusion.43
  1026.0 118.7 %all-gather.3.cloned.1.call-done = bf16[8,1728,320]{1,2,0:T(8,128)(2,1)} async-done(((bf16[1,1728,320]{1,2,0:T(8,128)(2,1)}), bf16[8,1728,320]{1,2,0:T(8,128)(2,1)}) %all-gather.3.cloned.1.call-update) | async-done | bytes 8847376 | tf_op jit(solution)/shard_map/all_gather | solution.py:51
  1144.7 12.2 %copy.234 = bf16[8,1728,320]{1,0,2:T(8,128)(2,1)} copy(bf16[8,1728,320]{1,2,0:T(8,128)(2,1)} %all-gather.3.cloned.1.call-done) | data formatting | bytes 17694720 | tf_op jit(solution)/shard_map/all_gather | solution.py:51
  1157.0 15.5 %reshape.371 = bf16[13824,320]{0,1:T(8,128)(2,1)} reshape(bf16[8,1728,320]{1,0,2:T(8,128)(2,1)} %copy.234) | data formatting | bytes 17694720
  (210 shorter events, 131.6 us)
Async XLA Ops:
  6.5 1011.0 %copy-start = (bf16[320,1728]{1,0:T(8,128)(2,1)S(1)}, bf16[320,1728]{1,0:T(8,128)(2,1)}, u32[]{:S(2)}) copy-start(bf16[320,1728]{1,0:T(8,128)(2,1)} %param.5) | copy-start | bytes 3317764
  6.5 233.3 %all-reduce.9.cloned.1.call-start = ((), (), s32[]{:S(2)}) async-start(), calls=%async_computation.2 | async-start | bytes 12386304 | tf_op jit(solution)/shard_map/psum | solution.py:35
  89.3 749.0 %reduce-scatter.2.cloned.1.call-start = ((), (), s32[]{:S(2)}) async-start(), calls=%async_computation.3 | async-start | bytes 8355840 | tf_op jit(solution)/shard_map/reduce_scatter | solution.py:32
  95.5 825.7 %all-reduce.11.cloned.1.call-start = ((), (), s32[]{:S(2)}) async-start(), calls=%async_computation.4 | async-start | bytes 983040 | tf_op jit(solution)/shard_map/psum | solution.py:33
  260.6 2.6 copy-start.10
  286.7 25.6 %copy-start.19 = (f32[2,128,128]{2,1,0:T(8,128)}, f32[2,128,128]{2,1,0:T(8,128)S(1)}, u32[]{:S(2)}) copy-start(f32[2,128,128]{2,1,0:T(8,128)S(1)} %custom-call.94) | copy-start | bytes 393220
  392.9 22.1 %copy-start.22 = (f32[2,128,128]{2,1,0:T(8,128)}, f32[2,128,128]{2,1,0:T(8,128)S(1)}, u32[]{:S(2)}) copy-start(f32[2,128,128]{2,1,0:T(8,128)S(1)} %custom-call.98) | copy-start | bytes 393220
  417.2 135.1 %copy-start.20 = (f32[2,128,128]{2,1,0:T(8,128)S(1)}, f32[2,128,128]{2,1,0:T(8,128)}, u32[]{:S(2)}) copy-start(f32[2,128,128]{2,1,0:T(8,128)} %copy-done.19) | copy-start | bytes 393220
  417.2 135.1 %copy-start.21 = (f32[2,128,128]{2,1,0:T(8,128)S(1)}, f32[2,128,128]{2,1,0:T(8,128)}, u32[]{:S(2)}) copy-start(f32[2,128,128]{2,1,0:T(8,128)} %custom-call.96) | copy-start | bytes 393220
  471.2 81.1 %copy-start.23 = (f32[2,128,128]{2,1,0:T(8,128)S(1)}, f32[2,128,128]{2,1,0:T(8,128)}, u32[]{:S(2)}) copy-start(f32[2,128,128]{2,1,0:T(8,128)} %copy-done.22) | copy-start | bytes 393220
  596.3 3.7 copy-start.24
  600.0 2.6 copy-start.5
  625.0 146.5 %copy-start.17 = (f32[128,864]{0,1:T(8,128)S(1)}, f32[128,864]{0,1:T(8,128)}, u32[]{:S(2)}) copy-start(f32[128,864]{0,1:T(8,128)} %get-tuple-element.50) | copy-start | bytes 1327108
  765.9 35.3 %copy-start.13 = (f32[2,7,128,128]{2,3,1,0:T(8,128)}, f32[2,7,128,128]{2,3,1,0:T(8,128)S(1)}, u32[]{:S(2)}) copy-start(f32[2,7,128,128]{2,3,1,0:T(8,128)S(1)} %custom-call.107) | copy-start | bytes 2752516
  768.2 12.1 %copy-start.1 = (f32[2,128,864]{1,2,0:T(8,128)}, f32[2,128,864]{1,2,0:T(8,128)S(1)}, u32[]{:S(2)}) copy-start(f32[2,128,864]{1,2,0:T(8,128)S(1)} %get-tuple-element.84) | copy-start | bytes 2654212
  770.5 4.8 copy-start.16
  771.4 8.9 copy-start.6
  775.3 9.6 copy-start.8
  780.3 6.6 copy-start.11
  780.3 6.6 copy-start.15
  802.2 7.9 copy-start.14
  802.2 8.8 copy-start.12
  807.1 8.6 copy-start.9
  810.9 16.9 %copy-start.3 = (f32[2,128,864]{1,2,0:T(8,128)}, f32[2,128,864]{1,2,0:T(8,128)S(1)}, u32[]{:S(2)}) copy-start(f32[2,128,864]{1,2,0:T(8,128)S(1)} %fusion.128) | copy-start | bytes 2654212
  819.9 1.2 copy-start.7
  826.8 1.3 copy-start.2
  828.1 10.4 copy-start.4
  838.3 306.4 %all-gather.3.cloned.1.call-start = ((), (), s32[]{:S(2)}) async-start(), calls=%async_computation.5 | async-start | bytes 10321920 | tf_op jit(solution)/shard_map/all_gather | solution.py:51
  839.4 143.2 %copy-start.25 = (f32[128,64]{1,0:T(8,128)S(1)}, f32[128,64]{1,0:T(8,128)}, u32[]{:S(2)}) copy-start(f32[128,64]{1,0:T(8,128)} %pad_convert_fusion) | copy-start | bytes 98308
  839.7 174.5 %copy-start.18 = (f32[320,320]{0,1:T(8,128)S(1)}, f32[320,320]{0,1:T(8,128)}, u32[]{:S(2)}) copy-start(f32[320,320]{0,1:T(8,128)} %fusion.121) | copy-start | bytes 1228804
Sparse Core Ops, SparseCore 0:
  89.4 150.3 all-reduce.8
  242.3 93.0 reduce-scatter.1
  838.4 82.7 all-reduce.10
  1026.1 118.5 all-gather.2
where the time goes:
time: 1190 us; the launch traced here: 1180 us
  other arithmetic  549 us (46%)
  waiting for transfers between devices  336 us (28%)
  matrix products  120 us (10%)
  local copies, waits for them, and re-layouts  109 us (9%)
  blocking collectives  49.3 us (4%)
  between operations  16.6 us (1%)
    another operation x39, other arithmetic, damped_inverse(): lower = jnp.linalg.cholesky(factor + damping * identity)  349 us
    another operation x15, other arithmetic, damped_inverse(): jax.scipy.linalg.cho_solve((lower, True), target).astype(jnp.bfloat16)  177 us
    psum x1, waiting for transfers between devices, shards(): grad_factor = lax.psum(factor_blocks(unit_rows, BG), 'dp') / total_tokens  137 us
    all_gather x1, waiting for transfers between devices, shards(): return lax.all_gather(result, 'owner', axis=1, tiled=True)  119 us
    psum x1, waiting for transfers between devices, shards(): act_factor = lax.psum(partial_value, 'owner') / total_tokens  79.8 us
    another operation x36, matrix products, damped_inverse(): jax.scipy.linalg.cho_solve((lower, True), target).astype(jnp.bfloat16)  72.5 us
    all_to_all x1, blocking collectives, shards(): lax.all_to_all(output_grads, 'owner', split_axis=1, concat_axis=0, tiled=...  49.3 us
    unnamed x63, local copies, waits for them, and re-layouts  29.7 us
  transfers between devices with their start and end apart: 4, of which 3 were waited for; matrix products, arithmetic and copies ran while one was open for 52% of the time, Pallas kernels for 0%

commit v1 on v0

v1 whole, which is shorter than its diff:
```python
import functools
import jax, jax.numpy as jnp
from jax import lax
from jax.experimental import pallas as pl
from jax.experimental.pallas import tpu as pltpu
f32=jnp.float32; bf16=jnp.bfloat16
NB=128

def split3(x):
    h=x.astype(bf16); r=x-h.astype(f32)
    m=r.astype(bf16); l=(r-m.astype(f32)).astype(bf16)
    return h,m,l

def bc(x,j):
    return jnp.broadcast_to(x[j:j+1,:],(8,128))

def eliminate(chains):
    lane=lax.broadcasted_iota(jnp.int32,(8,128),1); sub=lax.broadcasted_iota(jnp.int32,(8,128),0)
    outs=[[] for _ in chains]
    for g in range(16):
        lo=8*g
        ing=(lane>=lo)&(lane<lo+8)
        eye=jnp.where(lane-lo==sub,1.0,0.0).astype(f32)
        st=[]
        for rows in chains:
            R=rows[g]
            B=[jnp.broadcast_to(R[:,lo+j:lo+j+1],(8,128)) for j in range(8)]
            st.append([jnp.where(ing,eye,R),B,jnp.zeros((8,128),f32)])
        for j in range(8):
            for s_ in st:
                R,B,U=s_
                p=bc(B[j],j)
                rs=lax.rsqrt(p)
                rs=rs*(1.5-0.5*p*rs*rs)
                inv=rs*rs
                m=bc(R,j)*inv
                U=jnp.where(sub==j,R*rs,U)
                R=jnp.where(sub==j,m,R-B[j]*m)
                for q in range(j+1,8):
                    s=bc(B[q],j)*inv
                    B[q]=jnp.where(sub==j,s,B[q]-B[j]*s)
                s_[0]=R; s_[2]=U
        for ci,(rows,s_) in enumerate(zip(chains,st)):
            W=s_[0]; outs[ci].append(s_[2])
            w=[bc(W,j) for j in range(8)]
            for i in range(g+1,16):
                a=rows[i]
                acc=jnp.where(ing,0.0,a)
                for j in range(8):
                    acc=acc-jnp.broadcast_to(a[:,lo+j:lo+j+1],(8,128))*w[j]
                rows[i]=acc
    return outs

def dot(a,b,ca,cb):
    return lax.dot_general(a,b,(((ca,),(cb,)),((),())),preferred_element_type=f32)

def load_diag(M,k):
    cols=pl.ds(pl.multiple_of(k*NB,NB),NB)
    return [M[pl.ds(pl.multiple_of(k*NB+8*i,8),8),cols] for i in range(16)]

def store_lower(LD,rows):
    lane=lax.broadcasted_iota(jnp.int32,(8,128),1); sub=lax.broadcasted_iota(jnp.int32,(8,128),0)
    for i,u in enumerate(rows):
        LD[8*i:8*i+8,:]=jnp.where(lane<=sub+8*i,u,0.0)

def panel(M,LD,k,n):
    nb=n//NB; r0=k*NB
    M[r0:r0+NB,r0:r0+NB]=jnp.where(lax.broadcasted_iota(jnp.int32,(NB,NB),0)==lax.broadcasted_iota(jnp.int32,(NB,NB),1),1.0,0.0).astype(f32)
    lh,lm,ll=split3(LD[...])
    mh,mm,ml=split3(M[r0:r0+NB,:])
    hm=jnp.concatenate([mh,mm],0); lhh=jnp.concatenate([ml,mh],0)
    U=dot(jnp.concatenate([lh,lh],1),hm,1,0)+dot(jnp.concatenate([lm,lm],1),hm,1,0)+dot(jnp.concatenate([lh,ll],1),lhh,1,0)
    M[r0:r0+NB,:]=U
    if k+1<nb:
        h,m,l=split3(U)
        c=r0+NB
        hm=jnp.concatenate([h,m],0); lhh=jnp.concatenate([l,h],0)
        ht,mt,lt=h[:,c:].T,m[:,c:].T,l[:,c:].T
        S=dot(jnp.concatenate([ht,ht],1),hm,1,0)+dot(jnp.concatenate([mt,mt],1),hm,1,0)+dot(jnp.concatenate([ht,lt],1),lhh,1,0)
        M[c:,r0:r0+NB]=jnp.zeros((n-c,NB),f32)
        M[c:,:]=M[c:,:]-S

def steps(M,LD,n,Ma,LDa,na,k0,k1):
    both=min(k1,na//NB) if Ma is not None else k0
    def body2(k,_):
        g,a=eliminate([load_diag(M,k),load_diag(Ma,k)])
        store_lower(LD,g); store_lower(LDa,a)
        for kk in range(k0,both):
            @pl.when(k==kk)
            def _():
                panel(M,LD,kk,n); panel(Ma,LDa,kk,na)
        return 0
    def body1(k,_):
        g,=eliminate([load_diag(M,k)])
        store_lower(LD,g)
        for kk in range(max(k0,both),k1):
            @pl.when(k==kk)
            def _(): panel(M,LD,kk,n)
        return 0
    if both>k0: lax.fori_loop(k0,both,body2,0)
    if k1>max(k0,both): lax.fori_loop(max(k0,both),k1,body1,0)


import itertools
import math
import numpy as np
from jax.sharding import Mesh, PartitionSpec as P

BA = 320
BG = 864
GP = 896
AP = 384
WIDE = BG + BA
DAMPING = 0.1
SIZES = dict(x=4, zl=2, c=2, y=4, zh=2)
GB = [(i, j) for i in range(GP // NB) for j in range(i, GP // NB)]
AB = [(i, j) for i in range(AP // NB) for j in range(i, AP // NB)]
ROWS = (len(GB) + len(AB)) * NB
CHUNK = ROWS // 8
VMEM = pltpu.CompilerParams(vmem_limit_bytes=56 << 20)


def move(a, names, target):
    dims = [SIZES[n] for n in names]
    pairs = []
    for at in itertools.product(*map(range, dims)):
        to = target(*at)
        pairs.append((int(np.ravel_multi_index(at, dims)), int(np.ravel_multi_index(to, dims))))
    return lax.ppermute(a, names, pairs)


def along_z(a, d):
    def target(zl, zh):
        z = (2 * zh + zl + d) % 4
        return z % 2, z // 2
    return move(a, ("zl", "zh"), target)


def along_y(a, d):
    return move(a, ("y",), lambda y: ((y + d) % 4,))


def swap_core(a):
    return move(a, ("c",), lambda c: (1 - c,))


def swap_zh(a):
    return move(a, ("zh",), lambda h: (1 - h,))


def in_plane(a, d, first):
    def target(x, c, y):
        return ((x + d) % 4, c, y) if (c == 0) == first else (x, c, (y + d) % 4)
    return move(a, ("x", "c", "y"), target)


def turn_kernel(g_ref, x_ref, o_ref):
    def put(ref, size, base):
        for t in range(ref.shape[1] // NB):
            tile = ref[:, t * NB:(t + 1) * NB].T
            at, end = t * NB, (t + 1) * NB
            while at < end:
                b = at // size
                stop = min(end, (b + 1) * size)
                o_ref[b, base + at - b * size:base + stop - b * size, :] = tile[at - t * NB:stop - t * NB, :]
                at = stop
    put(g_ref, BG, 0)
    put(x_ref, BA, BG)


def turn(g, x):
    return pl.pallas_call(
        turn_kernel,
        out_shape=jax.ShapeDtypeStruct((16, WIDE, NB), bf16),
        compiler_params=VMEM,
    )(g, x)


def gram_kernel(at_ref, t_ref, mine_ref, other_ref, g_ref, a_ref, p_ref):
    z, c = at_ref[0], at_ref[1]
    g_ref[BG:, :] = jnp.zeros((GP - BG, 16 * NB), bf16)
    a_ref[BA:, :] = jnp.zeros((AP - BA, 16 * NB), bf16)
    for s in range(16):
        g_ref[:BG, s * NB:(s + 1) * NB] = t_ref[s, :BG, :]
        a_ref[:BA, s * NB:(s + 1) * NB] = t_ref[s, BG:, :]

    def products(ref, n, blocks, base):
        for r0 in range(0, n, 2 * NB):
            rows = min(2 * NB, n - r0)
            d = dot(ref[r0:r0 + rows, :], ref[r0:, :], 1, 1)
            for k, (i, j) in enumerate(blocks):
                if r0 <= i * NB < r0 + rows:
                    p_ref[base + k * NB:base + (k + 1) * NB, :] = d[i * NB - r0:(i + 1) * NB - r0, j * NB - r0:(j + 1) * NB - r0]

    products(g_ref, GP, GB, 0)
    products(a_ref, AP, AB, len(GB) * NB)
    for q in range(4):
        d = lax.rem(q - z + 4, 4)
        rows = pl.ds(pl.multiple_of(d * CHUNK, 8), CHUNK)
        first, second = p_ref[q * CHUNK:(q + 1) * CHUNK, :], p_ref[(4 + q) * CHUNK:(5 + q) * CHUNK, :]
        mine_ref[rows, :] = jnp.where(c == 0, first, second)
        other_ref[rows, :] = jnp.where(c == 0, second, first)


def gram(at, t):
    half = jax.ShapeDtypeStruct((4 * CHUNK, NB), f32)
    return pl.pallas_call(
        gram_kernel,
        out_shape=(half, half),
        in_specs=[pl.BlockSpec(memory_space=pltpu.SMEM), pl.BlockSpec(memory_space=pltpu.VMEM)],
        scratch_shapes=[
            pltpu.VMEM((GP, 16 * NB), bf16),
            pltpu.VMEM((AP, 16 * NB), bf16),
            pltpu.VMEM((ROWS, NB), f32),
        ],
        compiler_params=VMEM,
    )(at, t)


def sum_over_copies(mine, other):
    h = mine + swap_core(other)
    part = [h[d * CHUNK:(d + 1) * CHUNK] for d in range(4)]
    got = [along_z(part[d], d) for d in (1, 2, 3)]
    s = part[0] + got[0] + got[1] + got[2]
    own = jnp.concatenate([s] + [along_z(s, d) for d in (1, 2, 3)], axis=0)
    return own, swap_core(own)


def eye(n):
    return jnp.where(
        lax.broadcasted_iota(jnp.int32, (n, n), 0) == lax.broadcasted_iota(jnp.int32, (n, n), 1), 1.0, 0.0
    ).astype(f32)


def first_kernel(at_ref, own_ref, part_ref, m_ref, t_ref, inv_ref, p_ref, LD, Ma, LDa):
    z, c = at_ref[0], at_ref[1]
    for d in range(4):
        q = lax.rem(z - d + 4, 4)
        p_ref[pl.ds(pl.multiple_of((4 * c + q) * CHUNK, 8), CHUNK), :] = own_ref[d * CHUNK:(d + 1) * CHUNK, :]
        p_ref[pl.ds(pl.multiple_of((4 * (1 - c) + q) * CHUNK, 8), CHUNK), :] = part_ref[d * CHUNK:(d + 1) * CHUNK, :]
    tokens = 16384.0

    def unpack(M, n, blocks, base):
        M[...] = jnp.zeros((n, n), f32)
        for k, (i, j) in enumerate(blocks):
            block = p_ref[base + k * NB:base + (k + 1) * NB, :] / tokens
            if i == j:
                block = block + DAMPING * eye(NB)
            M[i * NB:(i + 1) * NB, j * NB:(j + 1) * NB] = block

    unpack(m_ref, GP, GB, 0)
    unpack(Ma, AP, AB, len(GB) * NB)
    steps(m_ref, LD, GP, Ma, LDa, AP, 0, 4)
    rows = pl.ds(pl.multiple_of(c * NB, NB), NB)
    t_ref[:, :256] = m_ref[rows, :256].astype(bf16)
    t_ref[:, 256:] = m_ref[pl.ds(pl.multiple_of(256 + c * NB, NB), NB), :512].astype(bf16)
    keep = lax.broadcasted_iota(jnp.int32, (NB, NB), 0) >= lax.broadcasted_iota(jnp.int32, (NB, NB), 1)
    @pl.when(c == 0)
    def _():
        t_ref[:, 0:128] = jnp.where(keep, t_ref[:, 0:128], 0)
        t_ref[:, 128:256] = jnp.zeros((NB, NB), bf16)
        t_ref[:, 512:640] = jnp.where(keep, t_ref[:, 512:640], 0)
        t_ref[:, 640:768] = jnp.zeros((NB, NB), bf16)

    @pl.when(c == 1)
    def _():
        t_ref[:, 128:256] = jnp.where(keep, t_ref[:, 128:256], 0)
        t_ref[:, 640:768] = jnp.where(keep, t_ref[:, 640:768], 0)

    n = AP // NB
    for i in range(n):
        Ma[i * NB:(i + 1) * NB, i * NB:(i + 1) * NB] = jnp.where(keep, Ma[i * NB:(i + 1) * NB, i * NB:(i + 1) * NB], 0.0)
        for j in range(i + 1, n):
            Ma[i * NB:(i + 1) * NB, j * NB:(j + 1) * NB] = jnp.zeros((NB, NB), f32)
    L = Ma[:BA, :BA]
    inv_ref[...] = lax.dot_general(
        L, L, (((0,), (0,)), ((), ())), precision=lax.Precision.HIGHEST, preferred_element_type=f32
    ).astype(bf16)


def first_inverse(at, own, part):
    return pl.pallas_call(
        first_kernel,
        out_shape=(
            jax.ShapeDtypeStruct((GP, GP), f32),
            jax.ShapeDtypeStruct((NB, 768), bf16),
            jax.ShapeDtypeStruct((BA, BA), bf16),
        ),
        in_specs=[pl.BlockSpec(memory_space=pltpu.SMEM)] + [pl.BlockSpec(memory_space=pltpu.VMEM)] * 2,
        scratch_shapes=[
            pltpu.VMEM((ROWS, NB), f32),
            pltpu.VMEM((NB, NB), f32),
            pltpu.VMEM((AP, AP), f32),
            pltpu.VMEM((NB, NB), f32),
        ],
        compiler_params=VMEM,
    )(at, own, part)


def second_kernel(at_ref, m_in, t_ref, M, LD, s_ref):
    c = at_ref[1]
    M[...] = m_in[...]
    steps(M, LD, GP, None, None, 0, 4, 7)
    keep = lax.broadcasted_iota(jnp.int32, (NB, NB), 0) >= lax.broadcasted_iota(jnp.int32, (NB, NB), 1)

    def diag(i):
        return jnp.where(keep, M[i * NB:(i + 1) * NB, i * NB:(i + 1) * NB], 0.0).astype(bf16)

    s_ref[:256, :512] = M[512:768, :512].astype(bf16)
    s_ref[:NB, 512:640] = diag(4)
    s_ref[:NB, 640:768] = jnp.zeros((NB, NB), bf16)
    s_ref[NB:256, 512:640] = M[640:768, 512:640].astype(bf16)
    s_ref[NB:256, 640:768] = diag(5)
    s_ref[256:352, :] = M[768:BG, :768].astype(bf16)
    last = diag(6)
    for j in range(6):
        s_ref[352:368, j * NB:(j + 1) * NB] = last[16 * j:16 * j + 16, :]
    s_ref[368:, :] = jnp.zeros((16, 768), bf16)
    t_ref[...] = s_ref[pl.ds(pl.multiple_of(c * 192, 16), 192), :]


def second_inverse(at, m):
    return pl.pallas_call(
        second_kernel,
        out_shape=jax.ShapeDtypeStruct((192, 768), bf16),
        in_specs=[pl.BlockSpec(memory_space=pltpu.SMEM), pl.BlockSpec(memory_space=pltpu.VMEM)],
        scratch_shapes=[pltpu.VMEM((GP, GP), f32), pltpu.VMEM((NB, NB), f32), pltpu.VMEM((384, 768), bf16)],
        compiler_params=VMEM,
    )(at, m)


def spread(t):
    q = jnp.stack([t] + [in_plane(t, d, True) for d in (1, 2, 3)])
    return jnp.stack([q] + [in_plane(q, d, False) for d in (1, 2, 3)])


def apply_kernel(idx_ref, l_ref, a1, b1, a2, b2, o_ref, s1, s2, lv):
    b = pl.program_id(0)
    c = idx_ref[3 * 16]

    @pl.when(b == 0)
    def _():
        lv[...] = jnp.zeros(lv.shape, bf16)

    s1[pl.ds(pl.multiple_of(c * 128, 128), 128), :] = a1[0]
    s1[pl.ds(pl.multiple_of((1 - c) * 128, 128), 128), :] = b1[0]
    s2[pl.ds(pl.multiple_of(c * 192, 16), 192), :] = a2[0]
    s2[pl.ds(pl.multiple_of((1 - c) * 192, 16), 192), :] = b2[0]
    lv[0:256, 0:256] = s1[:, 0:256]
    lv[256:512, 0:512] = s1[:, 256:768]
    lv[512:864, 0:768] = s2[0:352, :]
    for j in range(6):
        lv[768 + 16 * j:784 + 16 * j, 768:896] = s2[352:368, j * NB:(j + 1) * NB]
    left = l_ref[0]
    y = [
        dot(left[:, :n], lv[r0:r1, :n], 1, 1).astype(bf16)
        for r0, r1, n in ((0, 256, 256), (256, 512, 512), (512, 768, 768), (768, 864, 864))
    ]
    out = []
    for i, (c0, c1) in enumerate(((0, 256), (256, 512), (512, 768), (768, 864))):
        acc = dot(y[i], lv[(0, 256, 512, 768)[i]:(256, 512, 768, 864)[i], c0:c1], 1, 0)
        for k in range(i + 1, 4):
            acc = acc + dot(y[k], lv[(0, 256, 512, 768)[k]:(256, 512, 768, 864)[k], c0:c1], 1, 0)
        out.append(acc.astype(bf16))
    for i in range(4):
        @pl.when(lax.rem(b, 4) == i)
        def _():
            for (c0, c1), v in zip(((0, 256), (256, 512), (512, 768), (768, 864)), out):
                o_ref[:, i * BG + c0:i * BG + c1] = v


def apply(idx, left, one, one_other, two, two_other):
    return pl.pallas_call(
        apply_kernel,
        out_shape=jax.ShapeDtypeStruct((BA, 16 * BG), bf16),
        grid_spec=pltpu.PrefetchScalarGridSpec(
            num_scalar_prefetch=1,
            grid=(16,),
            in_specs=[
                pl.BlockSpec((1, BA, BG), lambda b, s: (s[b], 0, 0)),
                pl.BlockSpec((1, 128, 768), lambda b, s: (s[16 + b], 0, 0)),
                pl.BlockSpec((1, 128, 768), lambda b, s: (s[32 + b], 0, 0)),
                pl.BlockSpec((1, 192, 768), lambda b, s: (s[16 + b], 0, 0)),
                pl.BlockSpec((1, 192, 768), lambda b, s: (s[32 + b], 0, 0)),
            ],
            out_specs=pl.BlockSpec((BA, 4 * BG), lambda b, s: (0, b // 4)),
            scratch_shapes=[
                pltpu.VMEM((256, 768), bf16),
                pltpu.VMEM((384, 768), bf16),
                pltpu.VMEM((BG, GP), bf16),
            ],
        ),
        compiler_params=VMEM,
    )(idx, left, one, one_other, two, two_other)


def shards(layer_inputs, output_grads, weight_grad):
    x, y, zh, zl, c = (lax.axis_index(n) for n in ("x", "y", "zh", "zl", "c"))
    at = jnp.stack([2 * zh + zl, c]).astype(jnp.int32)
    w = weight_grad.reshape(BA, 2, BG).transpose(1, 0, 2)
    w = jnp.concatenate([w, swap_zh(w)], axis=0)
    w = jnp.concatenate([w] + [along_y(w, d) for d in (1, 2, 3)], axis=0)

    t = turn(output_grads, layer_inputs)
    t = lax.all_to_all(t, ("x", "y"), 0, 0, tiled=True)
    mine, other = gram(at, t)
    own, part = sum_over_copies(mine, other)
    m, t1, act = first_inverse(at, own, part)
    act = move(
        act, ("zl", "c", "y"), lambda zl, c, y: (y >> 1, y & 1, 2 * zl + c)
    )
    one = spread(t1).reshape(16, 128, 768)
    one_other = swap_core(one)
    t2 = second_inverse(at, m)
    two = spread(t2).reshape(16, 192, 768)
    two_other = swap_core(two)
    left = lax.dot_general(act, w, (((1,), (1,)), ((), ())), preferred_element_type=f32).astype(bf16)
    left = left.transpose(1, 0, 2)
    b = jnp.arange(16)
    w_at = ((y - (b >> 2)) % 4) * 4 + (zh ^ ((b >> 1) & 1)) * 2 + (b & 1)
    dx, dy = (x - (b >> 2)) % 4, (y - (b & 3)) % 4
    by_x, by_y = dy * 4 + dx, dx * 4 + dy
    idx = jnp.concatenate([
        w_at, jnp.where(c == 0, by_x, by_y), jnp.where(c == 0, by_y, by_x), c[None]
    ]).astype(jnp.int32)
    return apply(idx, left, one, one_other, two, two_other)


def solution(mesh):
    fine = Mesh(np.asarray(mesh.devices).reshape(tuple(SIZES.values())), tuple(SIZES))
    dp, owner = ("x", "zl", "c"), ("y", "zh")
    return jax.shard_map(
        shards,
        mesh=fine,
        in_specs=(P(dp + owner, None), P(dp + owner, None), P(dp, owner)),
        out_specs=P(dp, None),
        check_vma=False,
    )
```

time: 1190 us -> 429 us (0.36)
  other arithmetic: 549 us -> 11.1 us
  waiting for transfers between devices: 336 us -> 216 us
  matrix products: 120 us -> 7.25 us
  Pallas kernels: 0 us -> 97.4 us
  local copies, waits for them, and re-layouts: 109 us -> 12 us
  starting transfers between devices: 0.76 us -> 77.6 us
  blocking collectives: 49.3 us -> 0 us
  between operations: 16.6 us -> 0.63 us
    another operation x54 -> x5, other arithmetic: 526 us -> 7.15 us  [the longest x4 6.5 us: spread(): return jnp.stack([q] + [in_plane(q, d, False) for d in (1, 2, 3)])]
    psum x2 -> x0, waiting for transfers between devices: 217 us -> none  [the longest x1 137 us: shards(): grad_factor = lax.psum(factor_blocks(unit_rows, BG), 'dp') / total_tokens]
    ppermute x0 -> x27, waiting for transfers between devices: none -> 144 us  [move(): return lax.ppermute(a, names, pairs)]
    all_gather x1 -> x0, waiting for transfers between devices: 119 us -> none  [shards(): return lax.all_gather(result, 'owner', axis=1, tiled=True)]
    another operation x52 -> x0, matrix products: 101 us -> none  [the longest x36 72.5 us: damped_inverse(): jax.scipy.linalg.cho_solve((lower, True), target).astype(jnp.bfloat16)]
    pallas_call x0 -> x5, Pallas kernels: none -> 97.4 us  [the longest x1 34.3 us: first_inverse(): pl.pallas_call(first_kernel, out_shape=(jax.ShapeDtypeStruct((GP, GP), f3...]
    all_to_all x0 -> x1, waiting for transfers between devices: none -> 72.4 us  [shards(): t = lax.all_to_all(t, ('x', 'y'), 0, 0, tiled=True)]
    ppermute x0 -> x27, starting transfers between devices: none -> 70.8 us  [move(): return lax.ppermute(a, names, pairs)]
  transfers between devices with their start and end apart: 4 -> 28, of which waited for: 3 -> 24; matrix products, arithmetic and copies ran while one was open for 52% -> 6% of each run, Pallas kernels for 0% -> 0%
where the time goes in v1:
time: 429 us; the launch traced here: 423 us
  waiting for transfers between devices  216 us (50%)
  Pallas kernels  97.4 us (23%)
  starting transfers between devices  77.6 us (18%)
  local copies, waits for them, and re-layouts  12 us (3%)
  other arithmetic  11.1 us (3%)
  matrix products  7.25 us (2%)
    ppermute x27, waiting for transfers between devices, move(): return lax.ppermute(a, names, pairs)  144 us
    all_to_all x1, waiting for transfers between devices, shards(): t = lax.all_to_all(t, ('x', 'y'), 0, 0, tiled=True)  72.4 us
    ppermute x27, starting transfers between devices, move(): return lax.ppermute(a, names, pairs)  70.8 us
    pallas_call x1, Pallas kernels, first_inverse(): pl.pallas_call(first_kernel, out_shape=(jax.ShapeDtypeStruct((GP, GP), f3...  34.3 us
    pallas_call x1, Pallas kernels, apply(): pl.pallas_call(apply_kernel, out_shape=jax.ShapeDtypeStruct((BA, 16 * BG)...  27.7 us
    pallas_call x1, Pallas kernels, second_inverse(): pl.pallas_call(second_kernel, out_shape=jax.ShapeDtypeStruct((192, 768),...  22.2 us
  transfers between devices with their start and end apart: 28, of which 24 were waited for; matrix products, arithmetic and copies ran while one was open for 6% of the time, Pallas kernels for 0%

profile of v1, /device:TPU:33, one launch (start us, length us, event | category | flops | bytes accessed | tf_op | source)
XLA Modules:
  0.0 422.5 jit_solution(7586164899940687986)
XLA Ops:
  0.0 5.9 %shard_map.37 = bf16[16,1184,128]{2,1,0:T(8,128)(2,1)} custom-call(bf16[128,13824]{1,0:T(8,128)(2,1)} %g_ref.1, bf16[128,5120]{1,0:T(8,128)(2,1)} %x_ref.1), custom_call_target="tpu_custom_call" | custom-call | tf_op jit(solution)/shard_map/pallas_call | solution.py:172
  5.9 6.8 %all-to-all-start = ((bf16[16,1184,128]{2,1,0:T(8,128)(2,1)}), bf16[16,1184,128]{2,1,0:T(8,128)(2,1)}, u32[]{:S(2)}, u32[]{:S(2)}) async-start(bf16[16,1184,128]{2,1,0:T(8,128)(2,1)} %shard_map.37), calls=%async_computation | async-start | bytes 9699328 | tf_op jit(solution)/shard_map/all_to_all | solution.py:405
  13.4 72.4 %all-to-all-done.t_ref = bf16[16,1184,128]{2,1,0:T(8,128)(2,1)} async-done(((bf16[16,1184,128]{2,1,0:T(8,128)(2,1)}), bf16[16,1184,128]{2,1,0:T(8,128)(2,1)}, u32[]{:S(2)}, u32[]{:S(2)}) %all-to-all-start) | async-done | bytes 4849696 | tf_op jit(solution)/shard_map/all_to_all | solution.py:405
  85.8 7.3 %shard_map.38 = (f32[2176,128]{1,0:T(8,128)}, f32[2176,128]{1,0:T(8,128)}) custom-call(s32[2]{0:T(128)} %pad_add_fusion.1.at_ref, bf16[16,1184,128]{2,1,0:T(8,128)(2,1)} %all-to-all-done.t_ref), custom_call_target="tpu_custom_call" | custom-call | tf_op jit(solution)/shard_map/pallas_call | solution.py:207
  93.1 2.5 collective-permute-start
  95.6 2.6 collective-permute-done
  99.7 2.8 collective-permute-start.2
  102.5 1.9 collective-permute-start.1
  104.4 3.5 collective-permute-done.3
  107.9 6.9 %collective-permute-done.2 = f32[544,128]{1,0:T(8,128)S(1)} collective-permute-done((f32[544,128]{1,0:T(8,128)S(1)}, f32[544,128]{1,0:T(8,128)S(1)}, u32[]{:S(2)}, u32[]{:S(2)}) %collective-permute-start.2) | collective-permute-done | bytes 278560 | tf_op jit(solution)/shard_map/ppermute | solution.py:129
  115.8 3.1 collective-permute-start.6
  120.2 3.9 collective-permute-done.6
  124.1 7.0 %collective-permute-done.5 = f32[544,128]{1,0:T(8,128)S(1)} collective-permute-done((f32[544,128]{1,0:T(8,128)S(1)}, f32[544,128]{1,0:T(8,128)S(1)}, u32[]{:S(2)}, u32[]{:S(2)}) %collective-permute-start.5) | collective-permute-done | bytes 278560 | tf_op jit(solution)/shard_map/ppermute | solution.py:129
  131.7 1.8 collective-permute-start.7
  133.5 2.4 collective-permute-done.7.part_ref
  136.9 34.3 %shard_map.39 = (f32[896,896]{1,0:T(8,128)}, bf16[128,768]{1,0:T(8,128)(2,1)}, bf16[320,320]{1,0:T(8,128)(2,1)}) custom-call(s32[2]{0:T(128)} %pad_add_fusion.1.at_ref, f32[2176,128]{1,0:T(8,128)} %copy-done.4, f32[2176,128]{1,0:T(8,128)} %copy-done.5), custom_call_target="tpu_custom_call" | custom-call | tf_op jit(solution)/shard_map/pallas_call | solution.py:282
  171.2 22.2 %shard_map.40 = bf16[192,768]{1,0:T(8,128)(2,1)} custom-call(s32[2]{0:T(128)} %pad_add_fusion.1.at_ref, f32[896,896]{1,0:T(8,128)} %get-tuple-element.14.m_in), custom_call_target="tpu_custom_call" | custom-call | tf_op jit(solution)/shard_map/pallas_call | solution.py:323
  193.4 1.5 collective-permute-start.20
  194.9 4.6 %collective-permute-done.22 = bf16[192,768]{1,0:T(8,128)(2,1)S(1)} collective-permute-done((bf16[192,768]{1,0:T(8,128)(2,1)}, bf16[192,768]{1,0:T(8,128)(2,1)S(1)}, u32[]{:S(2)}, u32[]{:S(2)}) %collective-permute-start.22) | collective-permute-done | bytes 294944 | tf_op jit(solution)/shard_map/ppermute | solution.py:129
  200.8 3.4 collective-permute-done.20
  204.1 2.2 fusion.10
  206.3 4.7 %collective-permute-start.25 = (bf16[4,192,768]{2,1,0:T(8,128)(2,1)}, bf16[4,192,768]{2,1,0:T(8,128)(2,1)S(1)}, u32[]{:S(2)}, u32[]{:S(2)}) collective-permute-start(bf16[4,192,768]{2,1,0:T(8,128)(2,1)} %get-tuple-element.16), channel_id=1, source_target_pairs={{0,6},{2,0},{4,2},{6,4},{8,104},{10,106},{12,108},{14,110},{32,38}... | collective-permute-start | bytes 3538952 | tf_op jit(solution)/shard_map/ppermute | solution.py:129
  211.0 4.0 collective-permute-start.24
  215.9 3.2 reshape.9
  219.2 2.4 collective-permute-start.9
  221.6 15.5 %collective-permute-done.25 = bf16[4,192,768]{2,1,0:T(8,128)(2,1)S(1)} collective-permute-done((bf16[4,192,768]{2,1,0:T(8,128)(2,1)}, bf16[4,192,768]{2,1,0:T(8,128)(2,1)S(1)}, u32[]{:S(2)}, u32[]{:S(2)}) %collective-permute-start.25) | collective-permute-done | bytes 1179680 | tf_op jit(solution)/shard_map/ppermute | solution.py:129
  237.1 4.8 %collective-permute-done.23 = bf16[4,192,768]{2,1,0:T(8,128)(2,1)} collective-permute-done((bf16[4,192,768]{2,1,0:T(8,128)(2,1)}, bf16[4,192,768]{2,1,0:T(8,128)(2,1)}, u32[]{:S(2)}, u32[]{:S(2)}) %collective-permute-start.23) | collective-permute-done | bytes 1179680 | tf_op jit(solution)/shard_map/ppermute | solution.py:129
  241.9 3.8 pad_maximum_fusion
  245.7 2.7 collective-permute-start.26
  250.1 3.1 collective-permute-done.15
  253.2 1.8 collective-permute-done.14
  255.0 2.1 collective-permute-done.13
  257.9 2.6 collective-permute-start.17
  261.1 1.8 pad_maximum_fusion.2
  262.9 5.6 %collective-permute-done.18 = bf16[4,128,768]{2,1,0:T(8,128)(2,1)S(1)} collective-permute-done((bf16[4,128,768]{2,1,0:T(8,128)(2,1)S(1)}, bf16[4,128,768]{2,1,0:T(8,128)(2,1)S(1)}, u32[]{:S(2)}, u32[]{:S(2)}) %collective-permute-start.18) | collective-permute-done | bytes 786464 | tf_op jit(solution)/shard_map/ppermute | solution.py:129
  270.9 8.1 %collective-permute-done.16 = bf16[4,128,768]{2,1,0:T(8,128)(2,1)S(1)} collective-permute-done((bf16[4,128,768]{2,1,0:T(8,128)(2,1)S(1)}, bf16[4,128,768]{2,1,0:T(8,128)(2,1)S(1)}, u32[]{:S(2)}, u32[]{:S(2)}) %collective-permute-start.16) | collective-permute-done | bytes 786464 | tf_op jit(solution)/shard_map/ppermute | solution.py:129
  279.4 14.1 %collective-permute-start.19 = (bf16[16,128,768]{2,1,0:T(8,128)(2,1)S(1)}, bf16[16,128,768]{2,1,0:T(8,128)(2,1)}, u32[]{:S(2)}, u32[]{:S(2)}) collective-permute-start(bf16[16,128,768]{2,1,0:T(8,128)(2,1)S(1)} %bitcast.33), channel_id=1, source_target_pairs={{0,8},{8,0},{1,9},{9,1},{2,10},{10,2},{3,11},{11,3},{4,12},{12,4},... | collective-permute-start | bytes 9437192 | tf_op jit(solution)/shard_map/ppermute | solution.py:129
  294.2 1.4 constant_dynamic-update-slice_fusion.4
  295.8 35.0 %collective-permute-done.10 = bf16[4,320,864]{2,1,0:T(8,128)(2,1)} collective-permute-done((bf16[4,320,864]{2,1,0:T(8,128)(2,1)}, bf16[4,320,864]{2,1,0:T(8,128)(2,1)}, u32[]{:S(2)}, u32[]{:S(2)}) %collective-permute-start.10) | collective-permute-done | bytes 2211872 | tf_op jit(solution)/shard_map/ppermute | solution.py:129
  330.8 2.0 constant_dynamic-update-slice_fusion.2
  332.8 20.4 %collective-permute-start.8 = (bf16[320,320]{1,0:T(8,128)(2,1)S(1)}, bf16[320,320]{1,0:T(8,128)(2,1)S(1)}, u32[]{:S(2)}, u32[]{:S(2)}) collective-permute-start(bf16[320,320]{1,0:T(8,128)(2,1)S(1)} %copy-done.7), channel_id=1, source_target_pairs={{0,0},{2,8},{4,16},{6,24},{8,2},{10,10},{12,18},{14,26},{16,4},{18... | collective-permute-start | bytes 614408 | tf_op jit(solution)/shard_map/ppermute | solution.py:129
  353.2 11.3 %collective-permute-done.11 = bf16[4,320,864]{2,1,0:T(8,128)(2,1)} collective-permute-done((bf16[4,320,864]{2,1,0:T(8,128)(2,1)}, bf16[4,320,864]{2,1,0:T(8,128)(2,1)}, u32[]{:S(2)}, u32[]{:S(2)}) %collective-permute-start.11) | collective-permute-done | bytes 2211872 | tf_op jit(solution)/shard_map/ppermute | solution.py:129
  364.5 2.0 constant_dynamic-update-slice_fusion.1
  366.5 12.8 %collective-permute-done.12 = bf16[4,320,864]{2,1,0:T(8,128)(2,1)} collective-permute-done((bf16[4,320,864]{2,1,0:T(8,128)(2,1)}, bf16[4,320,864]{2,1,0:T(8,128)(2,1)}, u32[]{:S(2)}, u32[]{:S(2)}) %collective-permute-start.12) | collective-permute-done | bytes 2211872 | tf_op jit(solution)/shard_map/ppermute | solution.py:129
  379.4 2.0 constant_dynamic-update-slice_fusion
  381.4 5.7 %collective-permute-done.8 = bf16[320,320]{1,0:T(8,128)(2,1)S(1)} collective-permute-done((bf16[320,320]{1,0:T(8,128)(2,1)S(1)}, bf16[320,320]{1,0:T(8,128)(2,1)S(1)}, u32[]{:S(2)}, u32[]{:S(2)}) %collective-permute-start.8) | collective-permute-done | bytes 204832 | tf_op jit(solution)/shard_map/ppermute | solution.py:129
  387.1 7.3 %convert_bitcast_fusion.l_ref = bf16[16,320,864]{2,1,0:T(8,128)(2,1)} fusion(bf16[16,320,864]{2,1,0:T(8,128)(2,1)S(1)} %constant_dynamic-update-slice_fusion, bf16[320,320]{1,0:T(8,128)(2,1)S(1)} %collective-permute-done.8), kind=kOutput, calls=%fused_computation | convolution fusion | flops 2835578880 | bytes 17899520 | tf_op jit(solution)/shard_map/dot_general | solution.py:417
  394.3 27.7 %shard_map.41 = bf16[320,13824]{1,0:T(8,128)(2,1)} custom-call(s32[49]{0:T(128)} %pad_add_fusion.idx_ref, bf16[16,320,864]{2,1,0:T(8,128)(2,1)} %convert_bitcast_fusion.l_ref, bf16[16,128,768]{2,1,0:T(8,128)(2,1)} %bitcast.34, bf16[16,128,768]{2,1,0:T(8,128)(2,1)} %collective-permute-done.19.b1, bf16[16,192,768]{2,1,0:T(8,128)(2,1)} %bitcast.22.a2, ...), custom_call_target="tpu_custom_call" | custom-call | tf_op jit(solution)/shard_map/pallas_call | solution.py:373
  (50 shorter events, 15.0 us)
Async XLA Ops:
  5.9 79.9 %all-to-all-start = ((bf16[16,1184,128]{2,1,0:T(8,128)(2,1)}), bf16[16,1184,128]{2,1,0:T(8,128)(2,1)}, u32[]{:S(2)}, u32[]{:S(2)}) async-start(bf16[16,1184,128]{2,1,0:T(8,128)(2,1)} %shard_map.37), calls=%async_computation | async-start | bytes 9699328 | tf_op jit(solution)/shard_map/all_to_all | solution.py:405
  93.1 5.1 %collective-permute-start = (f32[2176,128]{1,0:T(8,128)}, f32[2176,128]{1,0:T(8,128)S(1)}, u32[]{:S(2)}, u32[]{:S(2)}) collective-permute-start(f32[2176,128]{1,0:T(8,128)} %get-tuple-element.11), channel_id=1, source_target_pairs={{0,8},{8,0},{1,9},{9,1},{2,10},{10,2},{3,11},{11,3},{4,12},{12,4},... | collective-permute-start | bytes 3342344 | tf_op jit(solution)/shard_map/ppermute | solution.py:129
  99.6 8.3 %collective-permute-start.3 = (f32[544,128]{1,0:T(8,128)S(1)}, f32[544,128]{1,0:T(8,128)S(1)}, u32[]{:S(2)}, u32[]{:S(2)}) collective-permute-start(f32[544,128]{1,0:T(8,128)S(1)} %get-tuple-element.18), channel_id=1, source_target_pairs={{0,17},{1,16},{16,0},{17,1},{2,19},{3,18},{18,2},{19,3},{4,21},{5,... | collective-permute-start | bytes 835592 | tf_op jit(solution)/shard_map/ppermute | solution.py:129
  99.7 15.2 %collective-permute-start.2 = (f32[544,128]{1,0:T(8,128)S(1)}, f32[544,128]{1,0:T(8,128)S(1)}, u32[]{:S(2)}, u32[]{:S(2)}) collective-permute-start(f32[544,128]{1,0:T(8,128)S(1)} %get-tuple-element.19), channel_id=1, source_target_pairs={{0,1},{1,0},{16,17},{17,16},{2,3},{3,2},{18,19},{19,18},{4,5},{5,4... | collective-permute-start | bytes 835592 | tf_op jit(solution)/shard_map/ppermute | solution.py:129
  102.5 13.2 %collective-permute-start.1 = (f32[544,128]{1,0:T(8,128)S(1)}, f32[544,128]{1,0:T(8,128)S(1)}, u32[]{:S(2)}, u32[]{:S(2)}) collective-permute-start(f32[544,128]{1,0:T(8,128)S(1)} %get-tuple-element.17), channel_id=1, source_target_pairs={{0,16},{1,17},{16,1},{17,0},{2,18},{3,19},{18,3},{19,2},{4,20},{5,... | collective-permute-start | bytes 835592 | tf_op jit(solution)/shard_map/ppermute | solution.py:129
  115.8 8.3 %collective-permute-start.6 = (f32[544,128]{1,0:T(8,128)S(1)}, f32[544,128]{1,0:T(8,128)S(1)}, u32[]{:S(2)}, u32[]{:S(2)}) collective-permute-start(f32[544,128]{1,0:T(8,128)S(1)} %fusion.1), channel_id=1, source_target_pairs={{0,17},{1,16},{16,0},{17,1},{2,19},{3,18},{18,2},{19,3},{4,21},{5,... | collective-permute-start | bytes 835592 | tf_op jit(solution)/shard_map/ppermute | solution.py:129
  118.9 12.2 %collective-permute-start.5 = (f32[544,128]{1,0:T(8,128)S(1)}, f32[544,128]{1,0:T(8,128)S(1)}, u32[]{:S(2)}, u32[]{:S(2)}) collective-permute-start(f32[544,128]{1,0:T(8,128)S(1)} %fusion.1), channel_id=1, source_target_pairs={{0,1},{1,0},{16,17},{17,16},{2,3},{3,2},{18,19},{19,18},{4,5},{5,4... | collective-permute-start | bytes 835592 | tf_op jit(solution)/shard_map/ppermute | solution.py:129
  118.9 12.7 %collective-permute-start.4 = (f32[544,128]{1,0:T(8,128)S(1)}, f32[544,128]{1,0:T(8,128)S(1)}, u32[]{:S(2)}, u32[]{:S(2)}) collective-permute-start(f32[544,128]{1,0:T(8,128)S(1)} %fusion.1), channel_id=1, source_target_pairs={{0,16},{1,17},{16,1},{17,0},{2,18},{3,19},{18,3},{19,2},{4,20},{5,... | collective-permute-start | bytes 835592 | tf_op jit(solution)/shard_map/ppermute | solution.py:129
  131.7 4.2 copy-start.4
  131.7 4.2 collective-permute-start.7
  135.9 1.0 copy-start.5
  193.4 6.1 %collective-permute-start.22 = (bf16[192,768]{1,0:T(8,128)(2,1)}, bf16[192,768]{1,0:T(8,128)(2,1)S(1)}, u32[]{:S(2)}, u32[]{:S(2)}) collective-permute-start(bf16[192,768]{1,0:T(8,128)(2,1)} %shard_map.40), channel_id=1, source_target_pairs={{0,96},{2,98},{4,100},{6,102},{8,14},{10,8},{12,10},{14,12},{32,0}... | collective-permute-start | bytes 884744 | tf_op jit(solution)/shard_map/ppermute | solution.py:129
  193.4 7.4 %collective-permute-start.21 = (bf16[192,768]{1,0:T(8,128)(2,1)}, bf16[192,768]{1,0:T(8,128)(2,1)S(1)}, u32[]{:S(2)}, u32[]{:S(2)}) collective-permute-start(bf16[192,768]{1,0:T(8,128)(2,1)} %shard_map.40), channel_id=1, source_target_pairs={{0,64},{2,66},{4,68},{6,70},{8,12},{10,14},{12,8},{14,10},{32,96},... | collective-permute-start | bytes 884744 | tf_op jit(solution)/shard_map/ppermute | solution.py:129
  193.4 10.7 %collective-permute-start.20 = (bf16[192,768]{1,0:T(8,128)(2,1)}, bf16[192,768]{1,0:T(8,128)(2,1)S(1)}, u32[]{:S(2)}, u32[]{:S(2)}) collective-permute-start(bf16[192,768]{1,0:T(8,128)(2,1)} %shard_map.40), channel_id=1, source_target_pairs={{0,32},{2,34},{4,36},{6,38},{8,10},{10,12},{12,14},{14,8},{32,64},... | collective-permute-start | bytes 884744 | tf_op jit(solution)/shard_map/ppermute | solution.py:129
  206.3 30.8 %collective-permute-start.25 = (bf16[4,192,768]{2,1,0:T(8,128)(2,1)}, bf16[4,192,768]{2,1,0:T(8,128)(2,1)S(1)}, u32[]{:S(2)}, u32[]{:S(2)}) collective-permute-start(bf16[4,192,768]{2,1,0:T(8,128)(2,1)} %get-tuple-element.16), channel_id=1, source_target_pairs={{0,6},{2,0},{4,2},{6,4},{8,104},{10,106},{12,108},{14,110},{32,38}... | collective-permute-start | bytes 3538952 | tf_op jit(solution)/shard_map/ppermute | solution.py:129
  211.0 26.1 %collective-permute-start.24 = (bf16[4,192,768]{2,1,0:T(8,128)(2,1)}, bf16[4,192,768]{2,1,0:T(8,128)(2,1)}, u32[]{:S(2)}, u32[]{:S(2)}) collective-permute-start(bf16[4,192,768]{2,1,0:T(8,128)(2,1)} %get-tuple-element.16), channel_id=1, source_target_pairs={{0,4},{2,6},{4,0},{6,2},{8,72},{10,74},{12,76},{14,78},{32,36},{34... | collective-permute-start | bytes 3538952 | tf_op jit(solution)/shard_map/ppermute | solution.py:129
  215.0 26.8 %collective-permute-start.23 = (bf16[4,192,768]{2,1,0:T(8,128)(2,1)}, bf16[4,192,768]{2,1,0:T(8,128)(2,1)}, u32[]{:S(2)}, u32[]{:S(2)}) collective-permute-start(bf16[4,192,768]{2,1,0:T(8,128)(2,1)} %get-tuple-element.16), channel_id=1, source_target_pairs={{0,2},{2,4},{4,6},{6,0},{8,40},{10,42},{12,44},{14,46},{32,34},{34... | collective-permute-start | bytes 3538952 | tf_op jit(solution)/shard_map/ppermute | solution.py:129
  219.1 26.6 %copy-start.1 = (bf16[320,2,864]{2,1,0:T(2,128)(2,1)}, bf16[320,2,864]{2,1,0:T(2,128)(2,1)S(1)}, u32[]{:S(2)}) copy-start(bf16[320,2,864]{2,1,0:T(2,128)(2,1)S(1)} %reshape.9) | copy-start | bytes 3317764
  219.2 41.9 %collective-permute-start.9 = (bf16[2,320,864]{2,1,0:T(8,128)(2,1)S(1)}, bf16[2,320,864]{2,1,0:T(8,128)(2,1)S(1)}, u32[]{:S(2)}, u32[]{:S(2)}) collective-permute-start(bf16[2,320,864]{2,1,0:T(8,128)(2,1)S(1)} %bitcast.35), channel_id=1, source_target_pairs={{0,1},{1,0},{2,3},{3,2},{4,5},{5,4},{6,7},{7,6},{8,9},{9,8},{10,11... | collective-permute-start | bytes 3317768 | tf_op jit(solution)/shard_map/ppermute | solution.py:129
  241.9 6.5 %copy-start.6 = (bf16[128,768]{1,0:T(8,128)(2,1)S(1)}, bf16[128,768]{1,0:T(8,128)(2,1)}, u32[]{:S(2)}) copy-start(bf16[128,768]{1,0:T(8,128)(2,1)} %get-tuple-element.13) | copy-start | bytes 589828
  245.7 148.7 %collective-permute-start.26 = (bf16[16,192,768]{2,1,0:T(8,128)(2,1)}, bf16[16,192,768]{2,1,0:T(8,128)(2,1)}, u32[]{:S(2)}, u32[]{:S(2)}) collective-permute-start(bf16[16,192,768]{2,1,0:T(8,128)(2,1)} %bitcast.22.a2), channel_id=1, source_target_pairs={{0,8},{8,0},{1,9},{9,1},{2,10},{10,2},{3,11},{11,3},{4,12},{12,4},... | collective-permute-start | bytes 14155784 | tf_op jit(solution)/shard_map/ppermute | solution.py:129
  248.4 4.8 %collective-permute-start.15 = (bf16[128,768]{1,0:T(8,128)(2,1)S(1)}, bf16[128,768]{1,0:T(8,128)(2,1)S(1)}, u32[]{:S(2)}, u32[]{:S(2)}) collective-permute-start(bf16[128,768]{1,0:T(8,128)(2,1)S(1)} %copy-done.6), channel_id=1, source_target_pairs={{0,96},{2,98},{4,100},{6,102},{8,14},{10,8},{12,10},{14,12},{32,0}... | collective-permute-start | bytes 589832 | tf_op jit(solution)/shard_map/ppermute | solution.py:129
  248.7 6.3 %collective-permute-start.14 = (bf16[128,768]{1,0:T(8,128)(2,1)S(1)}, bf16[128,768]{1,0:T(8,128)(2,1)S(1)}, u32[]{:S(2)}, u32[]{:S(2)}) collective-permute-start(bf16[128,768]{1,0:T(8,128)(2,1)S(1)} %copy-done.6), channel_id=1, source_target_pairs={{0,64},{2,66},{4,68},{6,70},{8,12},{10,14},{12,8},{14,10},{32,96},... | collective-permute-start | bytes 589832 | tf_op jit(solution)/shard_map/ppermute | solution.py:129
  249.6 7.6 %collective-permute-start.13 = (bf16[128,768]{1,0:T(8,128)(2,1)S(1)}, bf16[128,768]{1,0:T(8,128)(2,1)S(1)}, u32[]{:S(2)}, u32[]{:S(2)}) collective-permute-start(bf16[128,768]{1,0:T(8,128)(2,1)S(1)} %copy-done.6), channel_id=1, source_target_pairs={{0,32},{2,34},{4,36},{6,38},{8,10},{10,12},{12,14},{14,8},{32,64},... | collective-permute-start | bytes 589832 | tf_op jit(solution)/shard_map/ppermute | solution.py:129
  257.3 11.2 %collective-permute-start.18 = (bf16[4,128,768]{2,1,0:T(8,128)(2,1)S(1)}, bf16[4,128,768]{2,1,0:T(8,128)(2,1)S(1)}, u32[]{:S(2)}, u32[]{:S(2)}) collective-permute-start(bf16[4,128,768]{2,1,0:T(8,128)(2,1)S(1)} %get-tuple-element.21), channel_id=1, source_target_pairs={{0,6},{2,0},{4,2},{6,4},{8,104},{10,106},{12,108},{14,110},{32,38}... | collective-permute-start | bytes 2359304 | tf_op jit(solution)/shard_map/ppermute | solution.py:129
  257.9 12.7 %collective-permute-start.17 = (bf16[4,128,768]{2,1,0:T(8,128)(2,1)S(1)}, bf16[4,128,768]{2,1,0:T(8,128)(2,1)S(1)}, u32[]{:S(2)}, u32[]{:S(2)}) collective-permute-start(bf16[4,128,768]{2,1,0:T(8,128)(2,1)S(1)} %get-tuple-element.21), channel_id=1, source_target_pairs={{0,4},{2,6},{4,0},{6,2},{8,72},{10,74},{12,76},{14,78},{32,36},{34... | collective-permute-start | bytes 2359304 | tf_op jit(solution)/shard_map/ppermute | solution.py:129
  260.6 18.4 %collective-permute-start.16 = (bf16[4,128,768]{2,1,0:T(8,128)(2,1)S(1)}, bf16[4,128,768]{2,1,0:T(8,128)(2,1)S(1)}, u32[]{:S(2)}, u32[]{:S(2)}) collective-permute-start(bf16[4,128,768]{2,1,0:T(8,128)(2,1)S(1)} %get-tuple-element.21), channel_id=1, source_target_pairs={{0,2},{2,4},{4,6},{6,0},{8,40},{10,42},{12,44},{14,46},{32,34},{34... | collective-permute-start | bytes 2359304 | tf_op jit(solution)/shard_map/ppermute | solution.py:129
  261.1 1.8 copy-start.2
  262.9 67.9 %collective-permute-start.10 = (bf16[4,320,864]{2,1,0:T(8,128)(2,1)}, bf16[4,320,864]{2,1,0:T(8,128)(2,1)}, u32[]{:S(2)}, u32[]{:S(2)}) collective-permute-start(bf16[4,320,864]{2,1,0:T(8,128)(2,1)} %pad_maximum_fusion.2), channel_id=1, source_target_pairs={{0,2},{2,4},{4,6},{6,0},{1,3},{3,5},{5,7},{7,1},{8,10},{10,12},{12... | collective-permute-start | bytes 6635528 | tf_op jit(solution)/shard_map/ppermute | solution.py:129
  268.5 96.0 %collective-permute-start.11 = (bf16[4,320,864]{2,1,0:T(8,128)(2,1)}, bf16[4,320,864]{2,1,0:T(8,128)(2,1)}, u32[]{:S(2)}, u32[]{:S(2)}) collective-permute-start(bf16[4,320,864]{2,1,0:T(8,128)(2,1)} %pad_maximum_fusion.2), channel_id=1, source_target_pairs={{0,4},{2,6},{4,0},{6,2},{1,5},{3,7},{5,1},{7,3},{8,12},{10,14},{12... | collective-permute-start | bytes 6635528 | tf_op jit(solution)/shard_map/ppermute | solution.py:129
  270.6 108.8 %collective-permute-start.12 = (bf16[4,320,864]{2,1,0:T(8,128)(2,1)}, bf16[4,320,864]{2,1,0:T(8,128)(2,1)}, u32[]{:S(2)}, u32[]{:S(2)}) collective-permute-start(bf16[4,320,864]{2,1,0:T(8,128)(2,1)} %pad_maximum_fusion.2), channel_id=1, source_target_pairs={{0,6},{2,0},{4,2},{6,4},{1,7},{3,1},{5,3},{7,5},{8,14},{10,8},{12,... | collective-permute-start | bytes 6635528 | tf_op jit(solution)/shard_map/ppermute | solution.py:129
  279.4 16.4 %copy-start = (bf16[4,4,128,768]{3,2,1,0:T(8,128)(2,1)}, bf16[4,4,128,768]{3,2,1,0:T(8,128)(2,1)S(1)}, u32[]{:S(2)}) copy-start(bf16[4,4,128,768]{3,2,1,0:T(8,128)(2,1)S(1)} %pad_maximum_fusion.1) | copy-start | bytes 9437188
  279.4 114.9 %collective-permute-start.19 = (bf16[16,128,768]{2,1,0:T(8,128)(2,1)S(1)}, bf16[16,128,768]{2,1,0:T(8,128)(2,1)}, u32[]{:S(2)}, u32[]{:S(2)}) collective-permute-start(bf16[16,128,768]{2,1,0:T(8,128)(2,1)S(1)} %bitcast.33), channel_id=1, source_target_pairs={{0,8},{8,0},{1,9},{9,1},{2,10},{10,2},{3,11},{11,3},{4,12},{12,4},... | collective-permute-start | bytes 9437192 | tf_op jit(solution)/shard_map/ppermute | solution.py:129
  293.5 2.1 copy-start.3
  295.8 37.0 %copy-start.7 = (bf16[320,320]{1,0:T(8,128)(2,1)S(1)}, bf16[320,320]{1,0:T(8,128)(2,1)}, u32[]{:S(2)}) copy-start(bf16[320,320]{1,0:T(8,128)(2,1)} %get-tuple-element.12) | copy-start | bytes 614404
  332.8 54.3 %collective-permute-start.8 = (bf16[320,320]{1,0:T(8,128)(2,1)S(1)}, bf16[320,320]{1,0:T(8,128)(2,1)S(1)}, u32[]{:S(2)}, u32[]{:S(2)}) collective-permute-start(bf16[320,320]{1,0:T(8,128)(2,1)S(1)} %copy-done.7), channel_id=1, source_target_pairs={{0,0},{2,8},{4,16},{6,24},{8,2},{10,10},{12,18},{14,26},{16,4},{18... | collective-permute-start | bytes 614408 | tf_op jit(solution)/shard_map/ppermute | solution.py:129
